TPU v7x, 768 devices: a whole 4x8x12 slice. The times are simulated.
768 devices in a mesh: gx: 12 (over z), yz: 64 (over x, y, core).
Axes of the slice: x: 4, y: 8, z: 12, core: 2. Of those that a mesh axis runs over, the one named last changes fastest.
Arguments:
- tokens: bfloat16 [768, 18432], P(None, 'gx'), may hold values from -200 to 200
- qkv_weight: bfloat16 [18432, 6656], P('gx', 'yz'), may hold values from -0.046875 to 0.046875
- gate_weight: bfloat16 [18432, 36864], P('gx', 'yz'), may hold values from -0.046875 to 0.046875
- up_weight: bfloat16 [18432, 36864], P('gx', 'yz'), may hold values from -0.046875 to 0.046875
- out_weight: bfloat16 [6144, 18432], P(None, 'yz'), may hold values from -0.3125 to 0.3125
- key_cache: bfloat16 [768, 512, 256], P(('gx', 'yz')), may hold values from -2000 to 2000
- value_cache: bfloat16 [768, 512, 256], P(('gx', 'yz')), may hold values from -24 to 24
- lengths: int32 [768], P(('gx', 'yz')), may hold values from 2 to 512, as said below
Outputs:
- attended: bfloat16 [768, 18432], P('gx', 'yz')
- hidden: bfloat16 [768, 36864], P('gx', 'yz')
- new_kv: bfloat16 [768, 512], P(('gx', 'yz'))
Inputs may be any that keep to these rules, and one draw needn't show every extreme that they name: `lengths`: some sequence holds 512 earlier tokens and some other holds 2.
All inputs are finite; a program needn't handle non-finite values.
Results may differ from a plain program's by a relative error of at most 0.012.
The roundings to bfloat16 on the way count: a program that leaves them out, or rounds other values in their place, can miss the bound.
Values may be sent and summed in bfloat16 or wider, within the bound.
No kernel may reach another device: no remote copies, remote signals or barrier semaphores. Data moves between devices by JAX's collectives and lax.ppermute only.
A program may use at most 64 MiB of HBM per device.

v0:
```python
import jax
import jax.numpy as jnp
from jax import lax
from jax.sharding import PartitionSpec as P

D = 18432


EPS = 1e-06


def rotate(values, positions):
    half = values.shape[-1] // 2
    freq = 10000.0 ** (-jnp.arange(half, dtype=jnp.float32) / half)
    angle = positions.astype(jnp.float32)[..., None] * freq
    cosine = jnp.cos(angle)
    sine = jnp.sin(angle)
    first = values[..., :half]
    second = values[..., half:]
    return jnp.concatenate(
        [first * cosine - second * sine, second * cosine + first * sine], axis=-1
    )


def attend(features, key_cache, value_cache, lengths):
    seqs = features.shape[0]
    head_dim = key_cache.shape[2]
    query_width = features.shape[1] - 2 * head_dim
    heads = query_width // head_dim
    queries = features[:, :query_width].reshape(seqs, heads, head_dim)
    q_rot = rotate(queries.astype(jnp.float32), lengths[:, None]).astype(jnp.bfloat16)
    k_rot = rotate(
        features[:, query_width : query_width + head_dim].astype(jnp.float32), lengths
    ).astype(jnp.bfloat16)
    value_new = features[:, query_width + head_dim :]
    new_kv = jnp.concatenate([k_rot, value_new], axis=1)
    scale = head_dim ** (-0.5)
    own = jnp.einsum("shd,sd->sh", q_rot, k_rot, preferred_element_type=jnp.float32) * scale
    slots = key_cache.shape[1]
    scores = (
        jnp.einsum("shd,sjd->shj", q_rot, key_cache, preferred_element_type=jnp.float32) * scale
    )
    valid = jnp.arange(slots, dtype=jnp.int32)[None, :] < lengths[:, None]
    masked = jnp.where(valid[:, None, :], scores, -jnp.inf)
    top = jnp.maximum(jnp.max(masked, axis=-1), own)
    expo = jnp.exp(masked - top[..., None])
    expo_own = jnp.exp(own - top)
    total = jnp.sum(expo, axis=-1) + expo_own
    weights = (expo / total[..., None]).astype(jnp.bfloat16)
    weight_own = (expo_own / total).astype(jnp.bfloat16)
    context = jnp.einsum("shj,sjd->shd", weights, value_cache, preferred_element_type=jnp.float32)
    context = (
        context
        + weight_own.astype(jnp.float32)[..., None] * value_new.astype(jnp.float32)[:, None, :]
    )
    return (context.astype(jnp.bfloat16).reshape(seqs, query_width), new_kv)


def on_device(
    tokens, qkv_weight, gate_weight, up_weight, out_weight, key_cache, value_cache, lengths
):
    local_hidden = gate_weight.shape[1]
    both_weights = jnp.concatenate([gate_weight, up_weight], axis=1)
    projected = jnp.dot(tokens, qkv_weight, preferred_element_type=jnp.float32)
    squares = jnp.sum(jnp.square(tokens.astype(jnp.float32)), axis=1)
    summed_qkv, summed_squares = (
        lax.psum_scatter(projected, "gx", scatter_dimension=0, tiled=True),
        lax.psum_scatter(squares, "gx", scatter_dimension=0, tiled=True),
    )
    summed_ffn = lax.psum_scatter(
        jnp.dot(tokens, both_weights, preferred_element_type=jnp.float32),
        "gx",
        scatter_dimension=0,
        tiled=True,
    )
    inv_rms = lax.rsqrt(summed_squares / D + EPS)
    qkv = (summed_qkv * inv_rms[:, None]).astype(jnp.bfloat16)
    scaled_ffn = summed_ffn * inv_rms[:, None]
    hidden = (jax.nn.silu(scaled_ffn[:, :local_hidden]) * scaled_ffn[:, local_hidden:]).astype(
        jnp.bfloat16
    )
    features = lax.all_to_all(qkv, "yz", split_axis=0, concat_axis=1, tiled=True)
    context, new_kv = attend(features, key_cache, value_cache, lengths)
    attended = jnp.dot(
        lax.all_gather(context, "yz", axis=0, tiled=True),
        out_weight,
        preferred_element_type=jnp.float32,
    ).astype(jnp.bfloat16)
    return (attended, hidden, new_kv)


def solution(mesh):
    return jax.shard_map(
        on_device,
        mesh=mesh,
        in_specs=(
            P(None, "gx"),
            P("gx", "yz"),
            P("gx", "yz"),
            P("gx", "yz"),
            P(None, "yz"),
            P(("gx", "yz"), None, None),
            P(("gx", "yz"), None, None),
            P(("gx", "yz")),
        ),
        out_specs=(P("gx", "yz"), P("gx", "yz"), P(("gx", "yz"), None)),
        check_vma=False,
    )
```

profile of v0, /device:TPU:1, one launch (start us, length us, event | category | flops | bytes accessed | tf_op | source)
XLA Modules:
  0.0 170.3 jit_solution(3544652088492174896)
XLA Ops:
  7.2 0.0 copy-start
  7.2 0.0 reduce-scatter.5.cloned.1.call-start
  7.2 3.4 %fusion.31 = f32[768,104]{1,0:T(8,128)} fusion(bf16[768,1536]{1,0:T(8,128)(2,1)} %param.8, bf16[1536,104]{0,1:T(8,128)(2,1)} %param.9), kind=kOutput, calls=%fused_computation.58 | convolution fusion | flops 245366784 | bytes 2998272 | tf_op jit(solution)/shard_map/dot_general | solution.py:64
  10.6 0.0 reduce-scatter.5.cloned.1.call-update
  10.6 0.0 reduce-scatter.7.cloned.1.call-start
  10.7 7.5 %convolution_bitcast_fusion = f32[768,1152]{0,1:T(8,128)} fusion(bf16[768,1536]{1,0:T(8,128)(2,1)} %param.8, bf16[1536,576]{0,1:T(8,128)(2,1)} %param.11, bf16[1536,576]{0,1:T(8,128)(2,1)} %param.10), kind=kOutput, calls=%fused_computation.1 | convolution fusion | flops 2724986880 | bytes 9437184 | tf_op jit(solution)/shard_map/dot_general | solution.py:71
  18.2 5.2 %copy.18 = f32[768,1152]{1,0:T(8,128)} copy(f32[768,1152]{0,1:T(8,128)} %convolution_bitcast_fusion) | data formatting | bytes 7077888
  23.3 0.0 reduce-scatter.7.cloned.1.call-update
  24.0 1.3 dynamic-slice
  25.9 2.2 %multiply_reduce_fusion = f32[768]{0:T(1024)S(1)} fusion(bf16[768,1536]{1,0:T(8,128)(2,1)} %param.8), kind=kLoop, calls=%fused_computation | loop fusion | flops 3538176 | bytes 2362368 | tf_op jit(solution)/shard_map/reduce_sum | solution.py:65
  28.1 30.0 %all-reduce = f32[768]{0:T(1024)S(1)} all-reduce(f32[768]{0:T(1024)S(1)} %multiply_reduce_fusion), channel_id=3, replica_groups=mesh['gx'=12,'yz'=64] {'gx'}, use_global_device_ids=true, to_apply=%region_2.0.clone | all-reduce | flops 768 | bytes 6144
  58.1 0.1 fusion.19
  58.2 0.0 copy-start.1
  58.2 0.6 fusion.22
  58.8 8.8 %reduce-scatter.5.cloned.1.call-done = f32[64,104]{1,0:T(8,128)} async-done(((f32[768,104]{1,0:T(8,128)}), f32[64,104]{1,0:T(8,128)}) %reduce-scatter.5.cloned.1.call-update) | async-done | bytes 26640 | tf_op jit(solution)/shard_map/reduce_scatter | solution.py:67
  67.6 0.8 fusion.15
  68.4 0.6 copy.16
  69.1 18.5 %all-to-all-start = ((bf16[64,1,104]{2,1,0:T(2,128)(2,1)}), bf16[64,1,104]{2,1,0:T(2,128)(2,1)}, u32[]{:S(2)}, u32[]{:S(2)}) async-start(bf16[64,1,104]{2,1,0:T(2,128)(2,1)} %copy.16), calls=%async_computation.1 | async-start | bytes 65536 | tf_op jit(solution)/shard_map/all_to_all | solution.py:82
  87.6 0.6 iota_compare_fusion
  88.2 0.0 copy-done.1
  88.2 8.4 %all-to-all-done = bf16[64,1,104]{2,1,0:T(2,128)(2,1)} async-done(((bf16[64,1,104]{2,1,0:T(2,128)(2,1)}), bf16[64,1,104]{2,1,0:T(2,128)(2,1)}, u32[]{:S(2)}, u32[]{:S(2)}) %all-to-all-start) | async-done | bytes 13344 | tf_op jit(solution)/shard_map/all_to_all | solution.py:82
  96.6 0.9 reduce.4
  97.4 0.7 all_to_all.14
  98.2 1.4 fusion.12
  99.6 1.3 reshape.200
  100.9 0.7 fusion.28
  101.6 0.1 subtract_convert_fusion.1
  101.7 0.0 copy-start.3
  101.7 0.0 copy-start.4
  101.7 0.7 fusion.16
  102.5 0.0 copy-done.3
  102.5 0.0 copy-done.4
  102.5 1.3 fusion.29
  103.7 0.1 fusion.30
  103.9 0.2 fusion.11
  104.1 1.2 fusion.4
  105.2 0.6 reshape.202
  105.9 1.2 pad_maximum_fusion.3
  107.1 48.8 %all-gather = bf16[64,1,6144]{2,1,0:T(2,128)(2,1)S(1)} all-gather(bf16[1,1,6144]{2,1,0:T(2,128)(2,1)} %reshape.202), channel_id=1, replica_groups=mesh['gx'=12,'yz'=64] {'yz'}, dimensions={0}, use_global_device_ids=true | all-gather | bytes 798720 | tf_op jit(solution)/shard_map/all_gather | solution.py:85
  156.0 0.0 copy-done
  156.0 0.0 copy-start.2
  156.0 2.0 %convolution_convert_fusion = bf16[64,288]{1,0:T(8,128)(2,1)} fusion(bf16[6144,288]{0,1:T(8,128)(2,1)S(1)} %copy-done, bf16[64,1,6144]{2,1,0:T(2,128)(2,1)S(1)} %all-gather), kind=kOutput, calls=%fused_computation.5 | convolution fusion | flops 226510848 | bytes 4362240 | tf_op jit(solution)/shard_map/dot_general | solution.py:84
  157.9 0.0 reduce-scatter.7.cloned.1.call-done
  157.9 2.0 %copy.19 = f32[64,1152]{0,1:T(8,128)} copy(f32[64,1152]{1,0:T(8,128)} %reduce-scatter.7.cloned.1.call-done) | data formatting | bytes 589824
  159.9 0.0 copy-done.2
  159.9 1.1 broadcast_multiply_fusion
  161.1 0.7 fusion.8
  161.8 1.7 copy.17
  (3 shorter events, 0.0 us)
Async XLA Ops:
  7.2 148.8 %copy-start = (bf16[6144,288]{0,1:T(8,128)(2,1)S(1)}, bf16[6144,288]{0,1:T(8,128)(2,1)}, u32[]{:S(2)}) copy-start(bf16[6144,288]{0,1:T(8,128)(2,1)} %param.12) | copy-start | bytes 10616836
  7.2 60.4 %reduce-scatter.5.cloned.1.call-start = ((), (), s32[]{:S(2)}) async-start(), calls=%async_computation.3 | async-start | bytes 425984 | tf_op jit(solution)/shard_map/reduce_scatter | solution.py:67
  10.6 147.3 %reduce-scatter.7.cloned.1.call-start = ((), (), s32[]{:S(2)}) async-start(), calls=%async_computation.4 | async-start | bytes 3833856
  58.2 30.0 %copy-start.1 = (f32[64]{0:T(128)}, f32[64]{0:T(128)S(1)}, u32[]{:S(2)}) copy-start(f32[64]{0:T(128)S(1)} %fusion.19) | copy-start | bytes 772
  69.1 27.5 %all-to-all-start = ((bf16[64,1,104]{2,1,0:T(2,128)(2,1)}), bf16[64,1,104]{2,1,0:T(2,128)(2,1)}, u32[]{:S(2)}, u32[]{:S(2)}) async-start(bf16[64,1,104]{2,1,0:T(2,128)(2,1)} %copy.16), calls=%async_computation.1 | async-start | bytes 65536 | tf_op jit(solution)/shard_map/all_to_all | solution.py:82
  101.7 0.8 copy-start.3
  101.7 0.8 copy-start.4
  156.0 4.0 %copy-start.2 = (f32[64]{0:T(128)S(1)}, f32[64]{0:T(128)}, u32[]{:S(2)}) copy-start(f32[64]{0:T(128)} %copy-done.1) | copy-start | bytes 772
Sparse Core Ops, SparseCore 0:
  11.1 56.4 reduce-scatter.4
  71.1 65.3 reduce-scatter.6
where the time goes:
time: 171 us; the launch traced here: 170 us
  blocking collectives  78.8 us (46%)
  starting transfers between devices  18.6 us (11%)
  waiting for transfers between devices  17.2 us (10%)
  matrix products  15.4 us (9%)
  between operations  15.4 us (9%)
  local copies, waits for them, and re-layouts  13.5 us (8%)
  other arithmetic  11.4 us (7%)
    all_gather x1, blocking collectives, on_device(): lax.all_gather(context, 'yz', axis=0, tiled=True)  48.8 us
    unnamed x1, blocking collectives  30 us
    all_to_all x1, starting transfers between devices, on_device(): lax.all_to_all(qkv, 'yz', split_axis=0, concat_axis=1, tiled=True)  18.5 us
    unnamed x15, local copies, waits for them, and re-layouts  10.8 us
    reduce_scatter x1, waiting for transfers between devices, on_device(): lax.psum_scatter(projected, 'gx', scatter_dimension=0, tiled=True)  8.79 us
    all_to_all x1, waiting for transfers between devices, on_device(): lax.all_to_all(qkv, 'yz', split_axis=0, concat_axis=1, tiled=True)  8.4 us
    dot_general x1, matrix products, on_device(): jnp.dot(tokens, both_weights, preferred_element_type=jnp.float32)  7.5 us
  transfers between devices with their start and end apart: 3, of which 2 were waited for; matrix products, arithmetic and copies ran while one was open for 18% of the time, Pallas kernels for 0%

commit v1 on v0

v1 whole, which is shorter than its diff:
```python
import jax
import jax.numpy as jnp
from jax import lax
from jax.experimental import pallas as pl
from jax.experimental.pallas import tpu as pltpu
from jax.sharding import Mesh, PartitionSpec as P

D = 18432
EPS = 1e-06
HD = 256
HALF = HD // 2
HEADS = 24
SLOTS = 512
ROWS = 768
GX = 12
X, Y, C = 4, 8, 2
YZ = X * Y * C
SEQS = ROWS // GX
QKV = 104
FFN = 576
MAIN = 512
TAIL = FFN - MAIN
BLOCK = 128
F32 = jnp.float32
BF16 = jnp.bfloat16


def params(mib, **kw):
    return pltpu.CompilerParams(vmem_limit_bytes=mib * 1024 * 1024, **kw)


def vmem(*shape):
    return pl.BlockSpec(shape, lambda *_: (0,) * len(shape))


def project_kernel(tok_ref, qkv_ref, gate_ref, up_ref, ffn_ref, part_ref, mixed):
    @pl.when(pl.program_id(0) == 0)
    def _():
        mixed[...] = jnp.concatenate(
            [
                gate_ref[:, MAIN:],
                up_ref[:, MAIN:],
                qkv_ref[...],
                jnp.zeros((qkv_ref.shape[0], 128 - QKV), BF16),
            ],
            axis=1,
        )

    tok = tok_ref[...]
    wide = tok.astype(F32)
    squares = jnp.sum(wide * wide, axis=1, keepdims=True)
    both = jnp.dot(tok, mixed[...], preferred_element_type=F32)
    ffn_ref[:, :MAIN] = jnp.dot(tok, gate_ref[:, :MAIN], preferred_element_type=F32)
    ffn_ref[:, MAIN : 2 * MAIN] = jnp.dot(tok, up_ref[:, :MAIN], preferred_element_type=F32)
    ffn_ref[:, 2 * MAIN :] = both[:, :128]
    lane = lax.broadcasted_iota(jnp.int32, (BLOCK, 128), 1)
    part_ref[...] = jnp.where(lane == QKV, squares, both[:, 128:])


def project(tokens, qkv_weight, gate_weight, up_weight):
    depth = tokens.shape[1]
    return pl.pallas_call(
        project_kernel,
        grid=(ROWS // BLOCK,),
        in_specs=[
            pl.BlockSpec((BLOCK, depth), lambda i: (i, 0)),
            vmem(depth, QKV),
            vmem(depth, FFN),
            vmem(depth, FFN),
        ],
        out_specs=[
            pl.BlockSpec((BLOCK, 2 * FFN), lambda i: (i, 0)),
            pl.BlockSpec((BLOCK, 128), lambda i: (i, 0)),
        ],
        out_shape=[
            jax.ShapeDtypeStruct((ROWS, 2 * FFN), F32),
            jax.ShapeDtypeStruct((ROWS, 128), F32),
        ],
        scratch_shapes=[pltpu.VMEM((depth, 256), BF16)],
        compiler_params=params(28),
        name="project",
    )(tokens, qkv_weight, gate_weight, up_weight)


def norm_kernel(part_ref, out_ref, inv_ref):
    total = part_ref[0:SEQS, :]
    for k in range(1, GX):
        total = total + part_ref[k * SEQS : (k + 1) * SEQS, :]
    inv = lax.rsqrt(total[:, QKV : QKV + 1] / D + EPS)
    inv_ref[...] = jnp.broadcast_to(inv, (SEQS, 128))
    lane = lax.broadcasted_iota(jnp.int32, (SEQS, 128), 1)
    feats = jnp.where(lane < QKV, total * inv, 0.0).astype(BF16).astype(F32)
    me = (lax.axis_index("x") * Y + lax.axis_index("y")) * C + lax.axis_index("c")
    shift = lax.rem(me * QKV, 128)
    moved = pltpu.roll(feats, shift, 1)
    out_ref[:, :128] = jnp.where(lane >= shift, moved, 0.0).astype(BF16)
    out_ref[:, 128:] = jnp.where(lane < shift, moved, 0.0).astype(BF16)


def norm(part):
    return pl.pallas_call(
        norm_kernel,
        out_shape=[
            jax.ShapeDtypeStruct((SEQS, 256), BF16),
            jax.ShapeDtypeStruct((SEQS, 128), F32),
        ],
        compiler_params=params(8),
        name="norm",
    )(part)


def attend_kernel(len_ref, feat_ref, turn_ref, key_ref, value_ref, ctx_ref, kv_ref):
    length = len_ref[0]
    pad = 32
    feats = jnp.concatenate([feat_ref[:, :128], feat_ref[:, 128:]], axis=0)
    row = lax.broadcasted_iota(jnp.int32, (2 * pad, 2 * YZ), 0)
    col = lax.broadcasted_iota(jnp.int32, (2 * pad, 2 * YZ), 1)
    want = jnp.where(row < pad, 2 * row, 2 * (row - pad) + 1)
    source = jnp.where(col < YZ, col, col - YZ)
    have = ((source * QKV) >> 7) + jnp.where(col < YZ, 0, 1)
    pick = jnp.where(want == have, 1.0, 0.0).astype(BF16)
    halves = jnp.dot(pick, feats, preferred_element_type=F32)
    first = halves[:pad]
    second = halves[pad:]
    cosine = turn_ref[0:1, :]
    sine = turn_ref[1:2, :]
    turned = jnp.concatenate(
        [first * cosine - second * sine, second * cosine + first * sine], axis=1
    ).astype(BF16)
    wide = turned.astype(F32)
    key_new = wide[HEADS : HEADS + 1, :]
    value_new = jnp.concatenate(
        [first[HEADS + 1 : HEADS + 2, :], second[HEADS + 1 : HEADS + 2, :]], axis=1
    )
    scale = HD ** (-0.5)
    own = jnp.sum(wide * key_new, axis=1, keepdims=True) * scale
    scores = (
        lax.dot_general(
            turned, key_ref[0], (((1,), (1,)), ((), ())), preferred_element_type=F32
        )
        * scale
    )
    slot = lax.broadcasted_iota(jnp.int32, (pad, SLOTS), 1)
    masked = jnp.where(slot < length, scores, -jnp.inf)
    top = jnp.maximum(jnp.max(masked, axis=1, keepdims=True), own)
    expo = jnp.exp(masked - top)
    expo_own = jnp.exp(own - top)
    total = jnp.sum(expo, axis=1, keepdims=True) + expo_own
    weights = (expo / total).astype(BF16)
    weight_own = (expo_own / total).astype(BF16).astype(F32)
    context = jnp.dot(weights, value_ref[0], preferred_element_type=F32) + weight_own * value_new
    context = jnp.concatenate([context[:HEADS, :HALF], context[:HEADS, HALF:]], axis=0).astype(BF16)
    for k in range(X * Y):
        ctx_ref[k] = context
    kv_ref[...] = jnp.concatenate([key_new, value_new], axis=1).astype(BF16)


def attend(feats, turn, key_cache, value_cache, lengths):
    return pl.pallas_call(
        attend_kernel,
        in_specs=[pl.BlockSpec(memory_space=pltpu.SMEM)]
        + [pl.BlockSpec(memory_space=pltpu.VMEM)] * 4,
        out_specs=[pl.BlockSpec(memory_space=pltpu.VMEM)] * 2,
        out_shape=[
            jax.ShapeDtypeStruct((X * Y, 2 * HEADS, HALF), BF16),
            jax.ShapeDtypeStruct((1, 2 * HD), BF16),
        ],
        compiler_params=params(8),
        name="attend",
    )(lengths, feats, turn, key_cache, value_cache)


def output_kernel(ctx_ref, weight_ref, out_ref):
    flat = ctx_ref[...].reshape(YZ, 2 * HEADS * HALF)
    ordered = jnp.concatenate(
        [
            flat[:, (half * HEADS + head) * HALF : (half * HEADS + head + 1) * HALF]
            for head in range(HEADS)
            for half in range(2)
        ],
        axis=1,
    )
    out = jnp.dot(ordered, weight_ref[...], preferred_element_type=F32).astype(BF16)
    row = lax.broadcasted_iota(jnp.int32, (YZ, YZ), 0)
    col = lax.broadcasted_iota(jnp.int32, (YZ, YZ), 1)
    pick = jnp.where(col == (row % C) * (X * Y) + row // C, 1.0, 0.0).astype(BF16)
    out_ref[...] = jnp.dot(pick, out, preferred_element_type=F32).astype(BF16)


def output(context, out_weight):
    return pl.pallas_call(
        output_kernel,
        out_shape=jax.ShapeDtypeStruct((YZ, out_weight.shape[1]), BF16),
        compiler_params=params(20),
        name="output",
    )(context, out_weight)


def hidden_kernel(ffn_ref, inv_ref, out_ref):
    inv = inv_ref[:, 0:1]
    gate = ffn_ref[:, :MAIN] * inv
    up = ffn_ref[:, MAIN : 2 * MAIN] * inv
    out_ref[:, :MAIN] = (gate * lax.logistic(gate) * up).astype(BF16)
    last = ffn_ref[:, 2 * MAIN :] * inv
    tail = last * lax.logistic(last) * pltpu.roll(last, TAIL, 1)
    out_ref[:, MAIN:] = tail[:, :TAIL].astype(BF16)


def hidden_of(ffn, inv):
    return pl.pallas_call(
        hidden_kernel,
        out_shape=jax.ShapeDtypeStruct((SEQS, FFN), BF16),
        compiler_params=params(8),
        name="hidden",
    )(ffn, inv)


def on_device(
    tokens, qkv_weight, gate_weight, up_weight, out_weight, key_cache, value_cache, lengths
):
    freq = 10000.0 ** (-jnp.arange(HALF, dtype=F32) / HALF)
    angle = lengths.astype(F32)[:, None] * freq
    turn = jnp.concatenate([jnp.cos(angle), jnp.sin(angle)], axis=0)
    ffn, part = project(tokens, qkv_weight, gate_weight, up_weight)
    ffn = lax.psum_scatter(ffn, "gx", scatter_dimension=0, tiled=True)
    part = lax.all_to_all(part, "gx", 0, 0, tiled=True)
    feats, inv = norm(part)
    feats = lax.all_to_all(feats, ("x", "y", "c"), 0, 0, tiled=True)
    context, new_kv = attend(feats, turn, key_cache, value_cache, lengths)
    context = lax.all_to_all(context, ("x", "y"), 0, 0, tiled=True)
    context = lax.all_gather(context, "c", axis=0, tiled=True)
    attended = output(context, out_weight)
    hidden = hidden_of(ffn, inv)
    return (attended, hidden, new_kv)


def solution(mesh):
    fine = Mesh(mesh.devices.reshape(GX, X, Y, C), ("gx", "x", "y", "c"))
    yz = ("x", "y", "c")
    every = ("gx", "x", "y", "c")
    return jax.shard_map(
        on_device,
        mesh=fine,
        in_specs=(
            P(None, "gx"),
            P("gx", yz),
            P("gx", yz),
            P("gx", yz),
            P(None, yz),
            P(every, None, None),
            P(every, None, None),
            P(every),
        ),
        out_specs=(P("gx", yz), P("gx", yz), P(every, None)),
        check_vma=False,
    )
```

time: 171 us -> 121 us (0.71)
  blocking collectives: 78.8 us -> 5.35 us
  starting transfers between devices: 18.6 us -> 35 us
  waiting for transfers between devices: 17.2 us -> 32.6 us
  matrix products: 15.4 us -> 0 us
  other arithmetic: 11.4 us -> 0.71 us
  local copies, waits for them, and re-layouts: 13.5 us -> 23.6 us
  Pallas kernels: 0 us -> 8.57 us
    all_gather x1, blocking collectives: 48.8 us -> 5.35 us  [on_device(): context = lax.all_gather(context, 'c', axis=0, tiled=True)]
    unnamed x1 -> x0, blocking collectives: 30 us -> none
    all_to_all x1 -> x3, waiting for transfers between devices: 8.4 us -> 32.6 us  [the longest x1 17.9 us: on_device(): part = lax.all_to_all(part, 'gx', 0, 0, tiled=True)]
    all_to_all x1 -> x3, starting transfers between devices: 18.5 us -> 34.9 us  [the longest x1 15.8 us: on_device(): part = lax.all_to_all(part, 'gx', 0, 0, tiled=True)]
    dot_general x6 -> x0, matrix products: 15.4 us -> none  [the longest x1 7.5 us: on_device(): jnp.dot(tokens, both_weights, preferred_element_type=jnp.float32)]
    unnamed x15 -> x21, local copies, waits for them, and re-layouts: 10.8 us -> 23 us
    reduce_scatter x1, waiting for transfers between devices: 8.79 us -> 0.01 us  [on_device(): ffn = lax.psum_scatter(ffn, 'gx', scatter_dimension=0, tiled=True)]
    pallas_call x0 -> x5, Pallas kernels: none -> 8.57 us  [the longest x1 4.57 us: project(): pl.pallas_call(project_kernel, grid=(ROWS // BLOCK,), in_specs=[pl.BlockS...]
  transfers between devices with their start and end apart: 3 -> 4, of which waited for: 2 -> 3; matrix products, arithmetic and copies ran while one was open for 18% -> 7% of each run, Pallas kernels for 0% -> 3%
where the time goes in v1:
time: 121 us
  starting transfers between devices  35 us (29%)
  waiting for transfers between devices  32.6 us (27%)
  local copies, waits for them, and re-layouts  23.6 us (20%)
  between operations  14.8 us (12%)
  Pallas kernels  8.57 us (7%)
  blocking collectives  5.35 us (4%)
    unnamed x21, local copies, waits for them, and re-layouts  23 us
    all_to_all x1, waiting for transfers between devices, on_device(): part = lax.all_to_all(part, 'gx', 0, 0, tiled=True)  17.9 us
    all_to_all x1, starting transfers between devices, on_device(): part = lax.all_to_all(part, 'gx', 0, 0, tiled=True)  15.8 us
    all_to_all x1, starting transfers between devices, on_device(): feats = lax.all_to_all(feats, ('x', 'y', 'c'), 0, 0, tiled=True)  15.2 us
    all_to_all x1, waiting for transfers between devices, on_device(): feats = lax.all_to_all(feats, ('x', 'y', 'c'), 0, 0, tiled=True)  9.2 us
    all_to_all x1, waiting for transfers between devices, on_device(): context = lax.all_to_all(context, ('x', 'y'), 0, 0, tiled=True)  5.47 us
    all_gather x1, blocking collectives, on_device(): context = lax.all_gather(context, 'c', axis=0, tiled=True)  5.35 us
    pallas_call x1, Pallas kernels, project(): pl.pallas_call(project_kernel, grid=(ROWS // BLOCK,), in_specs=[pl.BlockS...  4.57 us
  transfers between devices with their start and end apart: 4, of which 3 were waited for; matrix products, arithmetic and copies ran while one was open for 7% of the time, Pallas kernels for 3%

profile of v1, /device:TPU:1, one launch (start us, length us, event | category | flops | bytes accessed | tf_op | source)
XLA Modules:
  0.0 120.5 jit_solution(14240929461049602404)
XLA Ops:
  7.2 0.0 reduce-scatter.2.cloned.1.call-start
  7.2 1.2 copy.20.qkv_ref
  8.4 2.7 %copy.21.gate_ref = bf16[1536,576]{1,0:T(8,128)(2,1)S(1)} copy(bf16[1536,576]{0,1:T(8,128)(2,1)} %param.10) | data formatting | bytes 3538944 | tf_op args[2]
  11.2 3.9 %copy.22.up_ref = bf16[1536,576]{1,0:T(8,128)(2,1)} copy(bf16[1536,576]{0,1:T(8,128)(2,1)} %param.11) | data formatting | bytes 3538944 | tf_op args[3]
  15.1 0.0 copy-start.1
  15.1 1.5 %copy-done.1 = bf16[1536,576]{1,0:T(8,128)(2,1)S(1)} copy-done((bf16[1536,576]{1,0:T(8,128)(2,1)S(1)}, bf16[1536,576]{1,0:T(8,128)(2,1)}, u32[]{:S(2)}) %copy-start.1) | copy-done | bytes 1769496
  16.6 0.0 copy-start.3
  16.6 1.7 %copy-done.3 = bf16[768,1536]{1,0:T(8,128)(2,1)S(1)} copy-done((bf16[768,1536]{1,0:T(8,128)(2,1)S(1)}, bf16[768,1536]{1,0:T(8,128)(2,1)}, u32[]{:S(2)}) %copy-start.3) | copy-done | bytes 2359320
  18.3 4.6 %project.1 = (f32[768,1152]{1,0:T(8,128)S(1)}, f32[768,128]{1,0:T(8,128)}) custom-call(bf16[768,1536]{1,0:T(8,128)(2,1)S(1)} %copy-done.3, bf16[1536,104]{1,0:T(8,128)(2,1)S(1)} %copy.20.qkv_ref, bf16[1536,576]{1,0:T(8,128)(2,1)S(1)} %copy.21.gate_ref, bf16[1536,576]{1,0:T(8,128)(2,1)S(1)} %copy-done.1), custom_call_target="tpu_custom_call" | custom-call | tf_op jit(solution)/shard_map/project/pallas_call | solution.py:62
  22.8 0.0 copy-start.2
  22.8 1.8 %copy-done.2 = f32[768,1152]{1,0:T(8,128)} copy-done((f32[768,1152]{1,0:T(8,128)}, f32[768,1152]{1,0:T(8,128)S(1)}, u32[]{:S(2)}) %copy-start.2) | copy-done | bytes 3538968
  24.6 0.0 copy-start.5
  24.6 0.0 copy-start.6
  24.6 0.0 reduce-scatter.2.cloned.1.call-update
  24.6 15.8 %all-to-all-start = ((f32[12,64,128]{2,1,0:T(8,128)}), f32[12,64,128]{2,1,0:T(8,128)S(1)}, u32[]{:S(2)}, u32[]{:S(2)}) async-start(f32[12,64,128]{2,1,0:T(8,128)} %bitcast), calls=%async_computation | async-start | bytes 786432 | tf_op jit(solution)/shard_map/all_to_all | solution.py:226
  41.1 0.1 fusion
  41.2 17.9 %all-to-all-done = f32[12,64,128]{2,1,0:T(8,128)S(1)} async-done(((f32[12,64,128]{2,1,0:T(8,128)}), f32[12,64,128]{2,1,0:T(8,128)S(1)}, u32[]{:S(2)}, u32[]{:S(2)}) %all-to-all-start) | async-done | bytes 393248 | tf_op jit(solution)/shard_map/all_to_all | solution.py:226
  59.1 0.2 norm.1
  59.3 0.5 broadcast.36
  59.8 0.7 reduce
  60.5 0.6 reshape.39
  61.1 15.2 %all-to-all-start.1 = ((bf16[64,2,128]{2,1,0:T(2,128)(2,1)}), bf16[64,2,128]{2,1,0:T(2,128)(2,1)S(1)}, u32[]{:S(2)}, u32[]{:S(2)}) async-start(bf16[64,2,128]{2,1,0:T(2,128)(2,1)} %reshape.39), calls=%async_computation.1 | async-start | bytes 65536 | tf_op jit(solution)/shard_map/all_to_all | solution.py:228
  76.3 9.2 %all-to-all-done.1 = bf16[64,2,128]{2,1,0:T(2,128)(2,1)S(1)} async-done(((bf16[64,2,128]{2,1,0:T(2,128)(2,1)}), bf16[64,2,128]{2,1,0:T(2,128)(2,1)S(1)}, u32[]{:S(2)}, u32[]{:S(2)}) %all-to-all-start.1) | async-done | bytes 32800 | tf_op jit(solution)/shard_map/all_to_all | solution.py:228
  85.6 0.0 copy-done.5
  85.6 0.0 copy-done.6
  85.6 1.4 %attend.1 = (bf16[32,48,128]{2,1,0:T(8,128)(2,1)}, bf16[1,512]{1,0:T(2,128)(2,1)}) custom-call(s32[1]{0:T(128)S(6)} %copy.29.len_ref, bf16[64,256]{1,0:T(8,128)(2,1)S(1)} %bitcast.8, f32[2,128]{1,0:T(2,128)S(1)} %pad_maximum_fusion.turn_ref, bf16[1,512,256]{2,1,0:T(8,128)(2,1)S(1)} %copy-done.5, bf16[1,512,256]{2,1,0:T(8,128)(2,1)S(1)} %copy-done.6), custom_call_target="tpu_custom_call" | custom-call | tf_op jit(solution)/shard_map/attend/pallas_call | solution.py:159
  87.0 3.9 %all-to-all-start.2 = ((bf16[32,48,128]{2,1,0:T(8,128)(2,1)}), bf16[32,48,128]{2,1,0:T(8,128)(2,1)S(1)}, u32[]{:S(2)}, u32[]{:S(2)}) async-start(bf16[32,48,128]{2,1,0:T(8,128)(2,1)} %get-tuple-element.11), calls=%async_computation.2 | async-start | bytes 786432 | tf_op jit(solution)/shard_map/all_to_all | solution.py:230
  90.9 6.3 %copy.24.weight_ref = bf16[6144,288]{1,0:T(8,128)(2,1)} copy(bf16[6144,288]{0,1:T(8,128)(2,1)} %param.12) | data formatting | bytes 7077888 | tf_op args[4]
  97.1 5.5 %all-to-all-done.2 = bf16[32,48,128]{2,1,0:T(8,128)(2,1)S(1)} async-done(((bf16[32,48,128]{2,1,0:T(8,128)(2,1)}), bf16[32,48,128]{2,1,0:T(8,128)(2,1)S(1)}, u32[]{:S(2)}, u32[]{:S(2)}) %all-to-all-start.2) | async-done | bytes 393248 | tf_op jit(solution)/shard_map/all_to_all | solution.py:230
  102.6 5.3 %all_gather.3.ctx_ref = bf16[64,48,128]{2,1,0:T(8,128)(2,1)S(1)} all-gather(bf16[32,48,128]{2,1,0:T(8,128)(2,1)S(1)} %all-to-all-done.2), channel_id=1, replica_groups=mesh['gx'=12,'x'=4,'y'=8,'c'=2] {'c'}, dimensions={0}, use_global_device_ids=true | all-gather | bytes 1179648 | tf_op jit(solution)/shard_map/all_gather | solution.py:231
  107.9 0.0 copy-start
  107.9 2.3 %copy-done = bf16[6144,288]{1,0:T(8,128)(2,1)S(1)} copy-done((bf16[6144,288]{1,0:T(8,128)(2,1)S(1)}, bf16[6144,288]{1,0:T(8,128)(2,1)}, u32[]{:S(2)}) %copy-start) | copy-done | bytes 3538968
  110.3 1.7 %output.1 = bf16[64,288]{1,0:T(8,128)(2,1)} custom-call(bf16[64,48,128]{2,1,0:T(8,128)(2,1)S(1)} %all_gather.3.ctx_ref, bf16[6144,288]{1,0:T(8,128)(2,1)S(1)} %copy-done), custom_call_target="tpu_custom_call" | custom-call | tf_op jit(solution)/shard_map/output/pallas_call | solution.py:191
  111.9 0.0 reduce-scatter.2.cloned.1.call-done.ffn_ref
  111.9 0.0 copy-start.4
  111.9 1.0 copy-done.4
  112.9 0.8 hidden.1
  (3 shorter events, 0.0 us)
Async XLA Ops:
  7.2 104.8 %reduce-scatter.2.cloned.1.call-start = ((), (), s32[]{:S(2)}) async-start(), calls=%async_computation.4 | async-start | bytes 3833856 | tf_op jit(solution)/shard_map/reduce_scatter | solution.py:225
  15.1 1.5 %copy-start.1 = (bf16[1536,576]{1,0:T(8,128)(2,1)S(1)}, bf16[1536,576]{1,0:T(8,128)(2,1)}, u32[]{:S(2)}) copy-start(bf16[1536,576]{1,0:T(8,128)(2,1)} %copy.22.up_ref) | copy-start | bytes 5308420
  16.6 1.7 %copy-start.3 = (bf16[768,1536]{1,0:T(8,128)(2,1)S(1)}, bf16[768,1536]{1,0:T(8,128)(2,1)}, u32[]{:S(2)}) copy-start(bf16[768,1536]{1,0:T(8,128)(2,1)} %tok_ref.1) | copy-start | bytes 7077892
  22.8 1.8 %copy-start.2 = (f32[768,1152]{1,0:T(8,128)}, f32[768,1152]{1,0:T(8,128)S(1)}, u32[]{:S(2)}) copy-start(f32[768,1152]{1,0:T(8,128)S(1)} %get-tuple-element.12) | copy-start | bytes 10616836
  24.6 61.0 %copy-start.5 = (bf16[1,512,256]{2,1,0:T(8,128)(2,1)S(1)}, bf16[1,512,256]{2,1,0:T(8,128)(2,1)}, u32[]{:S(2)}) copy-start(bf16[1,512,256]{2,1,0:T(8,128)(2,1)} %key_ref.1) | copy-start | bytes 786436
  24.6 61.0 %copy-start.6 = (bf16[1,512,256]{2,1,0:T(8,128)(2,1)S(1)}, bf16[1,512,256]{2,1,0:T(8,128)(2,1)}, u32[]{:S(2)}) copy-start(bf16[1,512,256]{2,1,0:T(8,128)(2,1)} %value_ref.1) | copy-start | bytes 786436
  24.6 34.5 %all-to-all-start = ((f32[12,64,128]{2,1,0:T(8,128)}), f32[12,64,128]{2,1,0:T(8,128)S(1)}, u32[]{:S(2)}, u32[]{:S(2)}) async-start(f32[12,64,128]{2,1,0:T(8,128)} %bitcast), calls=%async_computation | async-start | bytes 786432 | tf_op jit(solution)/shard_map/all_to_all | solution.py:226
  61.1 24.4 %all-to-all-start.1 = ((bf16[64,2,128]{2,1,0:T(2,128)(2,1)}), bf16[64,2,128]{2,1,0:T(2,128)(2,1)S(1)}, u32[]{:S(2)}, u32[]{:S(2)}) async-start(bf16[64,2,128]{2,1,0:T(2,128)(2,1)} %reshape.39), calls=%async_computation.1 | async-start | bytes 65536 | tf_op jit(solution)/shard_map/all_to_all | solution.py:228
  87.0 15.6 %all-to-all-start.2 = ((bf16[32,48,128]{2,1,0:T(8,128)(2,1)}), bf16[32,48,128]{2,1,0:T(8,128)(2,1)S(1)}, u32[]{:S(2)}, u32[]{:S(2)}) async-start(bf16[32,48,128]{2,1,0:T(8,128)(2,1)} %get-tuple-element.11), calls=%async_computation.2 | async-start | bytes 786432 | tf_op jit(solution)/shard_map/all_to_all | solution.py:230
  107.9 2.3 %copy-start = (bf16[6144,288]{1,0:T(8,128)(2,1)S(1)}, bf16[6144,288]{1,0:T(8,128)(2,1)}, u32[]{:S(2)}) copy-start(bf16[6144,288]{1,0:T(8,128)(2,1)} %copy.24.weight_ref) | copy-start | bytes 10616836
  111.9 1.0 copy-start.4
Sparse Core Ops, SparseCore 0:
  24.8 70.2 reduce-scatter.1

commit v2 on v1

--- a/solution.py
+++ b/solution.py
@@ -33,40 +33,39 @@
     return pl.BlockSpec(shape, lambda *_: (0,) * len(shape))
 
 
+def dot_rows(left, right):
+    return lax.dot_general(left, right, (((1,), (1,)), ((), ())), preferred_element_type=F32)
+
+
 def project_kernel(tok_ref, qkv_ref, gate_ref, up_ref, ffn_ref, part_ref, mixed):
     @pl.when(pl.program_id(0) == 0)
     def _():
-        mixed[...] = jnp.concatenate(
-            [
-                gate_ref[:, MAIN:],
-                up_ref[:, MAIN:],
-                qkv_ref[...],
-                jnp.zeros((qkv_ref.shape[0], 128 - QKV), BF16),
-            ],
-            axis=1,
-        )
+        mixed[:TAIL] = gate_ref[MAIN:]
+        mixed[TAIL : 2 * TAIL] = up_ref[MAIN:]
+        fill = jnp.zeros((128 - QKV, qkv_ref.shape[1]), F32)
+        mixed[2 * TAIL :] = jnp.concatenate([qkv_ref[...].astype(F32), fill], axis=0).astype(BF16)
 
     tok = tok_ref[...]
     wide = tok.astype(F32)
     squares = jnp.sum(wide * wide, axis=1, keepdims=True)
-    both = jnp.dot(tok, mixed[...], preferred_element_type=F32)
-    ffn_ref[:, :MAIN] = jnp.dot(tok, gate_ref[:, :MAIN], preferred_element_type=F32)
-    ffn_ref[:, MAIN : 2 * MAIN] = jnp.dot(tok, up_ref[:, :MAIN], preferred_element_type=F32)
+    both = dot_rows(tok, mixed[...])
+    ffn_ref[:, :MAIN] = dot_rows(tok, gate_ref[:MAIN])
+    ffn_ref[:, MAIN : 2 * MAIN] = dot_rows(tok, up_ref[:MAIN])
     ffn_ref[:, 2 * MAIN :] = both[:, :128]
     lane = lax.broadcasted_iota(jnp.int32, (BLOCK, 128), 1)
     part_ref[...] = jnp.where(lane == QKV, squares, both[:, 128:])
 
 
-def project(tokens, qkv_weight, gate_weight, up_weight):
+def project(tokens, qkv_rows, gate_rows, up_rows):
     depth = tokens.shape[1]
     return pl.pallas_call(
         project_kernel,
         grid=(ROWS // BLOCK,),
         in_specs=[
             pl.BlockSpec((BLOCK, depth), lambda i: (i, 0)),
-            vmem(depth, QKV),
-            vmem(depth, FFN),
-            vmem(depth, FFN),
+            vmem(QKV, depth),
+            vmem(FFN, depth),
+            vmem(FFN, depth),
         ],
         out_specs=[
             pl.BlockSpec((BLOCK, 2 * FFN), lambda i: (i, 0)),
@@ -76,10 +75,10 @@
             jax.ShapeDtypeStruct((ROWS, 2 * FFN), F32),
             jax.ShapeDtypeStruct((ROWS, 128), F32),
         ],
-        scratch_shapes=[pltpu.VMEM((depth, 256), BF16)],
-        compiler_params=params(28),
+        scratch_shapes=[pltpu.VMEM((256, depth), BF16)],
+        compiler_params=params(56),
         name="project",
-    )(tokens, qkv_weight, gate_weight, up_weight)
+    )(tokens, qkv_rows, gate_rows, up_rows)
 
 
 def norm_kernel(part_ref, out_ref, inv_ref):
@@ -91,17 +90,14 @@
     lane = lax.broadcasted_iota(jnp.int32, (SEQS, 128), 1)
     feats = jnp.where(lane < QKV, total * inv, 0.0).astype(BF16).astype(F32)
     me = (lax.axis_index("x") * Y + lax.axis_index("y")) * C + lax.axis_index("c")
-    shift = lax.rem(me * QKV, 128)
-    moved = pltpu.roll(feats, shift, 1)
-    out_ref[:, :128] = jnp.where(lane >= shift, moved, 0.0).astype(BF16)
-    out_ref[:, 128:] = jnp.where(lane < shift, moved, 0.0).astype(BF16)
+    out_ref[...] = pltpu.roll(feats, lax.rem(me * QKV, 128), 1)
 
 
 def norm(part):
     return pl.pallas_call(
         norm_kernel,
         out_shape=[
-            jax.ShapeDtypeStruct((SEQS, 256), BF16),
+            jax.ShapeDtypeStruct((SEQS, 128), F32),
             jax.ShapeDtypeStruct((SEQS, 128), F32),
         ],
         compiler_params=params(8),
@@ -112,7 +108,12 @@
 def attend_kernel(len_ref, feat_ref, turn_ref, key_ref, value_ref, ctx_ref, kv_ref):
     length = len_ref[0]
     pad = 32
-    feats = jnp.concatenate([feat_ref[:, :128], feat_ref[:, 128:]], axis=0)
+    rolled = feat_ref[...]
+    start = (lax.broadcasted_iota(jnp.int32, (YZ, 128), 0) * QKV) & 127
+    wrapped = lax.broadcasted_iota(jnp.int32, (YZ, 128), 1) < start
+    feats = jnp.concatenate(
+        [jnp.where(wrapped, 0.0, rolled), jnp.where(wrapped, rolled, 0.0)], axis=0
+    ).astype(BF16)
     row = lax.broadcasted_iota(jnp.int32, (2 * pad, 2 * YZ), 0)
     col = lax.broadcasted_iota(jnp.int32, (2 * pad, 2 * YZ), 1)
     want = jnp.where(row < pad, 2 * row, 2 * (row - pad) + 1)
@@ -150,6 +151,10 @@
     weight_own = (expo_own / total).astype(BF16).astype(F32)
     context = jnp.dot(weights, value_ref[0], preferred_element_type=F32) + weight_own * value_new
     context = jnp.concatenate([context[:HEADS, :HALF], context[:HEADS, HALF:]], axis=0).astype(BF16)
+    row = lax.broadcasted_iota(jnp.int32, (2 * HEADS, 2 * HEADS), 0)
+    col = lax.broadcasted_iota(jnp.int32, (2 * HEADS, 2 * HEADS), 1)
+    weave = jnp.where(col == (row % 2) * HEADS + row // 2, 1.0, 0.0).astype(BF16)
+    context = jnp.dot(weave, context, preferred_element_type=F32).astype(BF16)
     for k in range(X * Y):
         ctx_ref[k] = context
     kv_ref[...] = jnp.concatenate([key_new, value_new], axis=1).astype(BF16)
@@ -172,28 +177,20 @@
 
 def output_kernel(ctx_ref, weight_ref, out_ref):
     flat = ctx_ref[...].reshape(YZ, 2 * HEADS * HALF)
-    ordered = jnp.concatenate(
-        [
-            flat[:, (half * HEADS + head) * HALF : (half * HEADS + head + 1) * HALF]
-            for head in range(HEADS)
-            for half in range(2)
-        ],
-        axis=1,
-    )
-    out = jnp.dot(ordered, weight_ref[...], preferred_element_type=F32).astype(BF16)
+    out = dot_rows(flat, weight_ref[...]).astype(BF16)
     row = lax.broadcasted_iota(jnp.int32, (YZ, YZ), 0)
     col = lax.broadcasted_iota(jnp.int32, (YZ, YZ), 1)
     pick = jnp.where(col == (row % C) * (X * Y) + row // C, 1.0, 0.0).astype(BF16)
     out_ref[...] = jnp.dot(pick, out, preferred_element_type=F32).astype(BF16)
 
 
-def output(context, out_weight):
+def output(context, out_rows):
     return pl.pallas_call(
         output_kernel,
-        out_shape=jax.ShapeDtypeStruct((YZ, out_weight.shape[1]), BF16),
+        out_shape=jax.ShapeDtypeStruct((YZ, out_rows.shape[0]), BF16),
         compiler_params=params(20),
         name="output",
-    )(context, out_weight)
+    )(context, out_rows)
 
 
 def hidden_kernel(ffn_ref, inv_ref, out_ref):
@@ -210,7 +207,7 @@
     return pl.pallas_call(
         hidden_kernel,
         out_shape=jax.ShapeDtypeStruct((SEQS, FFN), BF16),
-        compiler_params=params(8),
+        compiler_params=params(56),
         name="hidden",
     )(ffn, inv)
 
@@ -221,7 +218,7 @@
     freq = 10000.0 ** (-jnp.arange(HALF, dtype=F32) / HALF)
     angle = lengths.astype(F32)[:, None] * freq
     turn = jnp.concatenate([jnp.cos(angle), jnp.sin(angle)], axis=0)
-    ffn, part = project(tokens, qkv_weight, gate_weight, up_weight)
+    ffn, part = project(tokens, qkv_weight.T, gate_weight.T, up_weight.T)
     ffn = lax.psum_scatter(ffn, "gx", scatter_dimension=0, tiled=True)
     part = lax.all_to_all(part, "gx", 0, 0, tiled=True)
     feats, inv = norm(part)
@@ -229,7 +226,7 @@
     context, new_kv = attend(feats, turn, key_cache, value_cache, lengths)
     context = lax.all_to_all(context, ("x", "y"), 0, 0, tiled=True)
     context = lax.all_gather(context, "c", axis=0, tiled=True)
-    attended = output(context, out_weight)
+    attended = output(context, out_weight.T)
     hidden = hidden_of(ffn, inv)
     return (attended, hidden, new_kv)
 

time: 121 us -> 116 us (0.959)
  local copies, waits for them, and re-layouts: 23.6 us -> 3.13 us
  blocking collectives: 5.35 us -> 20.3 us
  Pallas kernels: 8.57 us -> 18.3 us
  waiting for transfers between devices: 32.6 us -> 27.2 us
  starting transfers between devices: 35 us -> 31.3 us
    unnamed x21 -> x10, local copies, waits for them, and re-layouts: 23 us -> 3.13 us
    all_to_all x0 -> x1, blocking collectives: none -> 14.6 us  [on_device(): context = lax.all_to_all(context, ('x', 'y'), 0, 0, tiled=True)]
    pallas_call x1, Pallas kernels: 4.57 us -> 11.7 us  [project(): pl.pallas_call(project_kernel, grid=(ROWS // BLOCK,), in_specs=[pl.BlockS...]
    all_to_all x1 -> x0, waiting for transfers between devices: 5.47 us -> none  [on_device(): context = lax.all_to_all(context, ('x', 'y'), 0, 0, tiled=True)]
    all_to_all x1 -> x0, starting transfers between devices: 3.88 us -> none  [on_device(): context = lax.all_to_all(context, ('x', 'y'), 0, 0, tiled=True)]
    pallas_call x2, Pallas kernels: 1.82 us -> 3.19 us  [the longest x1 2.02 us: output(): pl.pallas_call(output_kernel, out_shape=jax.ShapeDtypeStruct((YZ, out_row...]
  transfers between devices with their start and end apart: 4 -> 3, of which waited for: 3 -> 2; matrix products, arithmetic and copies ran while one was open for 7% -> 0% of each run, Pallas kernels for 3% -> 4%
where the time goes in v2:
time: 116 us; the launch traced here: 115 us
  starting transfers between devices  31.3 us (27%)
  waiting for transfers between devices  27.2 us (23%)
  blocking collectives  20.3 us (18%)
  Pallas kernels  18.3 us (16%)
  between operations  14.7 us (13%)
  local copies, waits for them, and re-layouts  3.13 us (3%)
    all_to_all x1, waiting for transfers between devices, on_device(): part = lax.all_to_all(part, 'gx', 0, 0, tiled=True)  18 us
    all_to_all x1, starting transfers between devices, on_device(): part = lax.all_to_all(part, 'gx', 0, 0, tiled=True)  16 us
    all_to_all x1, starting transfers between devices, on_device(): feats = lax.all_to_all(feats, ('x', 'y', 'c'), 0, 0, tiled=True)  15.3 us
    all_to_all x1, blocking collectives, on_device(): context = lax.all_to_all(context, ('x', 'y'), 0, 0, tiled=True)  14.6 us
    pallas_call x1, Pallas kernels, project(): pl.pallas_call(project_kernel, grid=(ROWS // BLOCK,), in_specs=[pl.BlockS...  11.7 us
    all_to_all x1, waiting for transfers between devices, on_device(): feats = lax.all_to_all(feats, ('x', 'y', 'c'), 0, 0, tiled=True)  9.13 us
    all_gather x1, blocking collectives, on_device(): context = lax.all_gather(context, 'c', axis=0, tiled=True)  5.7 us
    unnamed x10, local copies, waits for them, and re-layouts  3.13 us
  transfers between devices with their start and end apart: 3, of which 2 were waited for; matrix products, arithmetic and copies ran while one was open for 0% of the time, Pallas kernels for 4%

profile of v2, /device:TPU:1, one launch (start us, length us, event | category | flops | bytes accessed | tf_op | source)
XLA Modules:
  0.0 115.0 jit_solution(7705975649651560346)
XLA Ops:
  7.2 0.0 reduce-scatter.2.cloned.1.call-start
  7.2 11.7 %project.1 = (f32[768,1152]{1,0:T(8,128)}, f32[768,128]{1,0:T(8,128)}) custom-call(bf16[768,1536]{1,0:T(8,128)(2,1)} %tok_ref.1, bf16[104,1536]{1,0:T(8,128)(2,1)} %bitcast.16, bf16[576,1536]{1,0:T(8,128)(2,1)} %bitcast.13, bf16[576,1536]{1,0:T(8,128)(2,1)} %bitcast.14), custom_call_target="tpu_custom_call" | custom-call | tf_op jit(solution)/shard_map/project/pallas_call | solution.py:61
  18.9 0.0 reduce-scatter.2.cloned.1.call-update
  18.9 0.0 copy-start
  18.9 16.0 %all-to-all-start = ((f32[12,64,128]{2,1,0:T(8,128)}), f32[12,64,128]{2,1,0:T(8,128)}, u32[]{:S(2)}, u32[]{:S(2)}) async-start(f32[12,64,128]{2,1,0:T(8,128)} %bitcast.15), calls=%async_computation | async-start | bytes 786432 | tf_op jit(solution)/shard_map/all_to_all | solution.py:223
  35.6 0.1 fusion
  35.6 18.0 %all-to-all-done = f32[12,64,128]{2,1,0:T(8,128)} async-done(((f32[12,64,128]{2,1,0:T(8,128)}), f32[12,64,128]{2,1,0:T(8,128)}, u32[]{:S(2)}, u32[]{:S(2)}) %all-to-all-start) | async-done | bytes 393248 | tf_op jit(solution)/shard_map/all_to_all | solution.py:223
  53.7 1.2 %norm.1 = (f32[64,128]{1,0:T(8,128)S(1)}, f32[64,128]{1,0:T(8,128)S(1)}) custom-call(f32[768,128]{1,0:T(8,128)} %bitcast.4.part_ref), custom_call_target="tpu_custom_call" | custom-call | tf_op jit(solution)/shard_map/norm/pallas_call | solution.py:97
  54.9 0.0 copy-start.3
  54.9 0.6 copy-done.3
  55.5 0.0 copy-start.4
  55.5 0.6 copy-done.4
  56.1 15.3 %all-to-all-start.1 = ((f32[64,1,128]{2,1,0:T(1,128)}), f32[64,1,128]{2,1,0:T(1,128)}, u32[]{:S(2)}, u32[]{:S(2)}) async-start(f32[64,1,128]{2,1,0:T(1,128)} %bitcast.12), calls=%async_computation.1 | async-start | bytes 65536 | tf_op jit(solution)/shard_map/all_to_all | solution.py:225
  71.4 9.1 %all-to-all-done.1 = f32[64,1,128]{2,1,0:T(1,128)} async-done(((f32[64,1,128]{2,1,0:T(1,128)}), f32[64,1,128]{2,1,0:T(1,128)}, u32[]{:S(2)}, u32[]{:S(2)}) %all-to-all-start.1) | async-done | bytes 32800 | tf_op jit(solution)/shard_map/all_to_all | solution.py:225
  80.5 0.0 copy-start.1
  80.5 1.0 copy-done.1
  81.4 0.0 copy-start.2
  81.4 1.0 copy-done.2
  82.4 1.7 %attend.1 = (bf16[32,48,128]{2,1,0:T(8,128)(2,1)S(1)}, bf16[1,512]{1,0:T(2,128)(2,1)}) custom-call(s32[1]{0:T(128)S(6)} %copy.12.len_ref, f32[64,128]{1,0:T(8,128)} %bitcast.7.feat_ref, f32[2,128]{1,0:T(2,128)S(1)} %pad_maximum_fusion.turn_ref, bf16[1,512,256]{2,1,0:T(8,128)(2,1)S(1)} %copy-done.1, bf16[1,512,256]{2,1,0:T(8,128)(2,1)S(1)} %copy-done.2), custom_call_target="tpu_custom_call" | custom-call | tf_op jit(solution)/shard_map/attend/pallas_call | solution.py:164
  84.1 14.6 %all_to_all.27 = bf16[32,48,128]{2,1,0:T(8,128)(2,1)S(1)} all-to-all(bf16[32,48,128]{2,1,0:T(8,128)(2,1)S(1)} %get-tuple-element.11), channel_id=1, replica_groups=mesh['gx'=12,'x'=4,'y'=8,'c'=2] {'x','y'}, dimensions={0} | all-to-all | bytes 786432 | tf_op jit(solution)/shard_map/all_to_all | solution.py:227
  98.7 5.7 %all_gather.3.ctx_ref = bf16[64,48,128]{2,1,0:T(8,128)(2,1)S(1)} all-gather(bf16[32,48,128]{2,1,0:T(8,128)(2,1)S(1)} %all_to_all.27), channel_id=1, replica_groups=mesh['gx'=12,'x'=4,'y'=8,'c'=2] {'c'}, dimensions={0}, use_global_device_ids=true | all-gather | bytes 1179648 | tf_op jit(solution)/shard_map/all_gather | solution.py:228
  104.4 0.0 copy-done
  104.4 2.0 %output.1 = bf16[64,288]{1,0:T(8,128)(2,1)} custom-call(bf16[64,48,128]{2,1,0:T(8,128)(2,1)S(1)} %all_gather.3.ctx_ref, bf16[288,6144]{1,0:T(8,128)(2,1)S(1)} %bitcast.11), custom_call_target="tpu_custom_call" | custom-call | tf_op jit(solution)/shard_map/output/pallas_call | solution.py:188
  106.4 0.0 reduce-scatter.2.cloned.1.call-done.ffn_ref
  106.4 1.8 %hidden.1 = bf16[64,576]{1,0:T(8,128)(2,1)} custom-call(f32[64,1152]{1,0:T(8,128)} %reduce-scatter.2.cloned.1.call-done.ffn_ref, f32[64,128]{1,0:T(8,128)} %copy-done.3), custom_call_target="tpu_custom_call" | custom-call | tf_op jit(solution)/shard_map/hidden/pallas_call | solution.py:207
  (1 shorter events, 0.0 us)
Async XLA Ops:
  7.2 99.3 %reduce-scatter.2.cloned.1.call-start = ((), (), s32[]{:S(2)}) async-start(), calls=%async_computation.4 | async-start | bytes 3833856 | tf_op jit(solution)/shard_map/reduce_scatter | solution.py:222
  18.9 85.5 %copy-start = (bf16[6144,288]{0,1:T(8,128)(2,1)S(1)}, bf16[6144,288]{0,1:T(8,128)(2,1)}, u32[]{:S(2)}) copy-start(bf16[6144,288]{0,1:T(8,128)(2,1)} %param.12) | copy-start | bytes 10616836
  18.9 34.7 %all-to-all-start = ((f32[12,64,128]{2,1,0:T(8,128)}), f32[12,64,128]{2,1,0:T(8,128)}, u32[]{:S(2)}, u32[]{:S(2)}) async-start(f32[12,64,128]{2,1,0:T(8,128)} %bitcast.15), calls=%async_computation | async-start | bytes 786432 | tf_op jit(solution)/shard_map/all_to_all | solution.py:223
  54.9 0.6 copy-start.3
  55.5 0.6 copy-start.4
  56.1 24.4 %all-to-all-start.1 = ((f32[64,1,128]{2,1,0:T(1,128)}), f32[64,1,128]{2,1,0:T(1,128)}, u32[]{:S(2)}, u32[]{:S(2)}) async-start(f32[64,1,128]{2,1,0:T(1,128)} %bitcast.12), calls=%async_computation.1 | async-start | bytes 65536 | tf_op jit(solution)/shard_map/all_to_all | solution.py:225
  80.5 1.0 copy-start.1
  81.4 1.0 copy-start.2
Sparse Core Ops, SparseCore 0:
  19.0 70.5 reduce-scatter.1

commit v3 on v2

v3 whole, which is shorter than its diff:
```python
import jax
import jax.numpy as jnp
from jax import lax
from jax.experimental import pallas as pl
from jax.experimental.pallas import tpu as pltpu
from jax.sharding import Mesh, PartitionSpec as P

D = 18432
EPS = 1e-06
HD = 256
HALF = HD // 2
HEADS = 24
SLOTS = 512
ROWS = 768
GX = 12
X, Y, C = 4, 8, 2
YZ = X * Y * C
SEQS = ROWS // GX
QKV = 104
FFN = 576
MAIN = 512
TAIL = FFN - MAIN
WIDE = 256
BLOCK = 384
SMALL = 128
F32 = jnp.float32
BF16 = jnp.bfloat16
WIRE = BF16


def params(mib, **kw):
    return pltpu.CompilerParams(vmem_limit_bytes=mib * 1024 * 1024, **kw)


def dot_rows(left, right):
    return lax.dot_general(left, right, (((1,), (1,)), ((), ())), preferred_element_type=F32)


def fetch(source, target, sem):
    copy = pltpu.make_async_copy(source, target, sem)
    copy.start()
    return copy


def qkv_kernel(tok_hbm, qkv_hbm, part_hbm, tok, qkv, part, sem_in, sem_out):
    weight = fetch(qkv_hbm, qkv, sem_in.at[0])
    blocks = [pl.ds(i * SMALL, SMALL) for i in range(ROWS // SMALL)]
    loads = [fetch(tok_hbm.at[r], tok.at[r], sem_in.at[1 + i]) for i, r in enumerate(blocks)]
    weight.wait()
    fill = jnp.zeros((128 - QKV, qkv.shape[1]), F32)
    padded = jnp.concatenate([qkv[...].astype(F32), fill], axis=0).astype(BF16)
    lane = lax.broadcasted_iota(jnp.int32, (SMALL, 128), 1)
    stores = []
    for i, r in enumerate(blocks):
        loads[i].wait()
        wide = tok[r, :].astype(F32)
        squares = jnp.sum(wide * wide, axis=1, keepdims=True)
        part[r, :] = jnp.where(lane == QKV, squares, dot_rows(tok[r, :], padded))
        stores.append(fetch(part.at[r], part_hbm.at[r], sem_out.at[i]))
    for copy in stores:
        copy.wait()


def project_qkv(tokens, qkv_rows):
    depth = tokens.shape[1]
    steps = ROWS // SMALL
    return pl.pallas_call(
        qkv_kernel,
        in_specs=[pl.BlockSpec(memory_space=pltpu.HBM)] * 2,
        out_specs=pl.BlockSpec(memory_space=pltpu.HBM),
        out_shape=jax.ShapeDtypeStruct((ROWS, 128), F32),
        scratch_shapes=[
            pltpu.VMEM((ROWS, depth), BF16),
            pltpu.VMEM((QKV, depth), BF16),
            pltpu.VMEM((ROWS, 128), F32),
            pltpu.SemaphoreType.DMA((1 + steps,)),
            pltpu.SemaphoreType.DMA((steps,)),
        ],
        compiler_params=params(62),
        name="project_qkv",
    )(tokens, qkv_rows)


def ffn_kernel(tok_hbm, gate_hbm, up_hbm, ffn_hbm, tok, rows, ffn, sem_in, sem_out):
    loads = []
    for n in range(4):
        weight = (gate_hbm, up_hbm)[n // 2]
        loads.append(fetch(weight.at[pl.ds(n % 2 * WIDE, WIDE)], rows.at[n], sem_in.at[n]))
        if n == 0:
            blocks = [pl.ds(i * BLOCK, BLOCK) for i in range(ROWS // BLOCK)]
            tokens = [
                fetch(tok_hbm.at[r], tok.at[r], sem_in.at[6 + i]) for i, r in enumerate(blocks)
            ]
    last = [
        fetch(gate_hbm.at[pl.ds(MAIN, TAIL)], rows.at[4, pl.ds(0, TAIL)], sem_in.at[4]),
        fetch(up_hbm.at[pl.ds(MAIN, TAIL)], rows.at[4, pl.ds(TAIL, TAIL)], sem_in.at[5]),
    ]
    stores = []

    def put(r, columns):
        place = (r, pl.ds(*columns))
        stores.append(fetch(ffn.at[place], ffn_hbm.at[place], sem_out.at[len(stores)]))

    for n in range(4):
        loads[n].wait()
        for i, r in enumerate(blocks):
            if n == 0:
                tokens[i].wait()
            ffn[r, pl.ds(n * WIDE, WIDE)] = dot_rows(tok[r, :], rows[n]).astype(ffn.dtype)
            if n % 2 == 1:
                put(r, ((n - 1) * WIDE, 2 * WIDE))
    for copy in last:
        copy.wait()
    for r in blocks:
        ffn[r, pl.ds(2 * MAIN, 128)] = dot_rows(tok[r, :], rows[4, :128]).astype(ffn.dtype)
        put(r, (2 * MAIN, 128))
    for copy in stores:
        copy.wait()


def project_ffn(tokens, gate_rows, up_rows):
    depth = tokens.shape[1]
    steps = ROWS // BLOCK
    return pl.pallas_call(
        ffn_kernel,
        in_specs=[pl.BlockSpec(memory_space=pltpu.HBM)] * 3,
        out_specs=pl.BlockSpec(memory_space=pltpu.HBM),
        out_shape=jax.ShapeDtypeStruct((ROWS, 2 * FFN), WIRE),
        scratch_shapes=[
            pltpu.VMEM((ROWS, depth), BF16),
            pltpu.VMEM((5, WIDE, depth), BF16),
            pltpu.VMEM((ROWS, 2 * FFN), WIRE),
            pltpu.SemaphoreType.DMA((6 + steps,)),
            pltpu.SemaphoreType.DMA((3 * steps,)),
        ],
        compiler_params=params(62),
        cost_estimate=pl.CostEstimate(
            flops=4 * ROWS * depth * FFN, bytes_accessed=10_000_000, transcendentals=0
        ),
        name="project_ffn",
    )(tokens, gate_rows, up_rows)


def my_shift():
    me = (lax.axis_index("x") * Y + lax.axis_index("y")) * C + lax.axis_index("c")
    return lax.rem(me * QKV, 128)


def norm_kernel(part_ref, out_ref):
    total = part_ref[0:SEQS, :]
    for k in range(1, GX):
        total = total + part_ref[k * SEQS : (k + 1) * SEQS, :]
    inv = lax.rsqrt(total[:, QKV : QKV + 1] / D + EPS)
    lane = lax.broadcasted_iota(jnp.int32, (SEQS, 128), 1)
    feats = jnp.where(lane == QKV, inv, (total * inv).astype(BF16).astype(F32))
    out_ref[...] = pltpu.roll(feats, my_shift(), 1)


def norm(part):
    return pl.pallas_call(
        norm_kernel,
        out_shape=jax.ShapeDtypeStruct((SEQS, 128), F32),
        compiler_params=params(62),
        name="norm",
    )(part)


def attend_kernel(
    len_ref, feat_hbm, turn_hbm, key_hbm, value_hbm, ctx_hbm, kv_ref, feat, turn, key, value, ctx, sem_in, sem_out
):
    near = [fetch(feat_hbm, feat, sem_in.at[0]), fetch(turn_hbm, turn, sem_in.at[1])]
    keys = fetch(key_hbm.at[0], key, sem_in.at[2])
    values = fetch(value_hbm.at[0], value, sem_in.at[3])
    for copy in near:
        copy.wait()
    length = len_ref[0]
    pad = 32
    rolled = feat[...]
    start = (lax.broadcasted_iota(jnp.int32, (YZ, 128), 0) * QKV) & 127
    lane = lax.broadcasted_iota(jnp.int32, (YZ, 128), 1)
    here = (lane >= start) & (lane < start + QKV)
    beyond = lane < start + QKV - 128
    feats = jnp.concatenate(
        [jnp.where(here, rolled, 0.0), jnp.where(beyond, rolled, 0.0)], axis=0
    ).astype(BF16)
    row = lax.broadcasted_iota(jnp.int32, (2 * pad, 2 * YZ), 0)
    col = lax.broadcasted_iota(jnp.int32, (2 * pad, 2 * YZ), 1)
    want = jnp.where(row < pad, 2 * row, 2 * (row - pad) + 1)
    source = jnp.where(col < YZ, col, col - YZ)
    have = ((source * QKV) >> 7) + jnp.where(col < YZ, 0, 1)
    pick = jnp.where(want == have, 1.0, 0.0).astype(BF16)
    halves = jnp.dot(pick, feats, preferred_element_type=F32)
    first = halves[:pad]
    second = halves[pad:]
    cosine = turn[0:1, :]
    sine = turn[1:2, :]
    turned = jnp.concatenate(
        [first * cosine - second * sine, second * cosine + first * sine], axis=1
    ).astype(BF16)
    wide = turned.astype(F32)
    key_new = wide[HEADS : HEADS + 1, :]
    value_new = jnp.concatenate(
        [first[HEADS + 1 : HEADS + 2, :], second[HEADS + 1 : HEADS + 2, :]], axis=1
    )
    kv_ref[...] = jnp.concatenate([key_new, value_new], axis=1).astype(BF16)
    scale = HD ** (-0.5)
    own = jnp.sum(wide * key_new, axis=1, keepdims=True) * scale
    slot = lax.broadcasted_iota(jnp.int32, (pad, SLOTS), 1)
    keys.wait()
    scores = dot_rows(turned, key[...]) * scale
    masked = jnp.where(slot < length, scores, -jnp.inf)
    top = jnp.maximum(jnp.max(masked, axis=1, keepdims=True), own)
    expo = jnp.exp(masked - top)
    expo_own = jnp.exp(own - top)
    total = jnp.sum(expo, axis=1, keepdims=True) + expo_own
    weights = (expo / total).astype(BF16)
    weight_own = (expo_own / total).astype(BF16).astype(F32)
    values.wait()
    context = jnp.dot(weights, value[...], preferred_element_type=F32) + weight_own * value_new
    context = jnp.concatenate([context[:HEADS, :HALF], context[:HEADS, HALF:]], axis=0).astype(BF16)
    row = lax.broadcasted_iota(jnp.int32, (2 * HEADS, 2 * HEADS), 0)
    col = lax.broadcasted_iota(jnp.int32, (2 * HEADS, 2 * HEADS), 1)
    weave = jnp.where(col == (row % 2) * HEADS + row // 2, 1.0, 0.0).astype(BF16)
    ctx[...] = jnp.dot(weave, context, preferred_element_type=F32).astype(BF16)
    stores = [fetch(ctx, ctx_hbm.at[k], sem_out.at[k]) for k in range(X * Y)]
    for copy in stores:
        copy.wait()


def attend(feats, turn, key_cache, value_cache, lengths):
    return pl.pallas_call(
        attend_kernel,
        in_specs=[pl.BlockSpec(memory_space=pltpu.SMEM)]
        + [pl.BlockSpec(memory_space=pltpu.HBM)] * 4,
        out_specs=[
            pl.BlockSpec(memory_space=pltpu.HBM),
            pl.BlockSpec(memory_space=pltpu.VMEM),
        ],
        out_shape=[
            jax.ShapeDtypeStruct((X * Y, 2 * HEADS, HALF), BF16),
            jax.ShapeDtypeStruct((1, 2 * HD), BF16),
        ],
        scratch_shapes=[
            pltpu.VMEM((YZ, 128), F32),
            pltpu.VMEM((2, HALF), F32),
            pltpu.VMEM((SLOTS, HD), BF16),
            pltpu.VMEM((SLOTS, HD), BF16),
            pltpu.VMEM((2 * HEADS, HALF), BF16),
            pltpu.SemaphoreType.DMA((4,)),
            pltpu.SemaphoreType.DMA((X * Y,)),
        ],
        compiler_params=params(62),
        name="attend",
    )(lengths, feats, turn, key_cache, value_cache)


def output_kernel(ctx_ref, rows_ref, out_ref):
    flat = ctx_ref[...].reshape(YZ, 2 * HEADS * HALF)
    out = dot_rows(flat, rows_ref[...]).astype(BF16)
    row = lax.broadcasted_iota(jnp.int32, (YZ, YZ), 0)
    col = lax.broadcasted_iota(jnp.int32, (YZ, YZ), 1)
    pick = jnp.where(col == (row % C) * (X * Y) + row // C, 1.0, 0.0).astype(BF16)
    out_ref[...] = jnp.dot(pick, out, preferred_element_type=F32).astype(BF16)


def output(context, out_rows):
    return pl.pallas_call(
        output_kernel,
        out_shape=jax.ShapeDtypeStruct((YZ, out_rows.shape[0]), BF16),
        compiler_params=params(20),
        name="output",
    )(context, out_rows)


def hidden_kernel(ffn_ref, feat_ref, out_ref):
    lane = lax.broadcasted_iota(jnp.int32, (SEQS, 128), 1)
    spare = lax.rem(my_shift() + QKV, 128)
    inv = jnp.sum(jnp.where(lane == spare, feat_ref[...], 0.0), axis=1, keepdims=True)
    gate = ffn_ref[:, :MAIN].astype(F32) * inv
    up = ffn_ref[:, MAIN : 2 * MAIN].astype(F32) * inv
    out_ref[:, :MAIN] = (gate * lax.logistic(gate) * up).astype(BF16)
    last = ffn_ref[:, 2 * MAIN :].astype(F32) * inv
    tail = last * lax.logistic(last) * pltpu.roll(last, TAIL, 1)
    out_ref[:, MAIN:] = tail[:, :TAIL].astype(BF16)


def hidden_of(ffn, feats):
    return pl.pallas_call(
        hidden_kernel,
        out_shape=jax.ShapeDtypeStruct((SEQS, FFN), BF16),
        compiler_params=params(62),
        name="hidden",
    )(ffn, feats)


def on_device(
    tokens, qkv_weight, gate_weight, up_weight, out_weight, key_cache, value_cache, lengths
):
    freq = 10000.0 ** (-jnp.arange(HALF, dtype=F32) / HALF)
    angle = lengths.astype(F32)[:, None] * freq
    turn = jnp.concatenate([jnp.cos(angle), jnp.sin(angle)], axis=0)
    part = project_qkv(tokens, qkv_weight.T)
    part = lax.all_to_all(part, "gx", 0, 0, tiled=True)
    ffn = project_ffn(tokens, gate_weight.T, up_weight.T)
    ffn = lax.psum_scatter(ffn, "gx", scatter_dimension=0, tiled=True)
    mine = norm(part)
    feats = lax.all_to_all(mine, ("x", "y", "c"), 0, 0, tiled=True)
    context, new_kv = attend(feats, turn, key_cache, value_cache, lengths)
    context = lax.all_to_all(context, ("x", "y"), 0, 0, tiled=True)
    context = lax.all_gather(context, "c", axis=0, tiled=True)
    attended = output(context, out_weight.T)
    hidden = hidden_of(ffn, mine)
    return (attended, hidden, new_kv)


def solution(mesh):
    fine = Mesh(mesh.devices.reshape(GX, X, Y, C), ("gx", "x", "y", "c"))
    yz = ("x", "y", "c")
    every = ("gx", "x", "y", "c")
    return jax.shard_map(
        on_device,
        mesh=fine,
        in_specs=(
            P(None, "gx"),
            P("gx", yz),
            P("gx", yz),
            P("gx", yz),
            P(None, yz),
            P(every, None, None),
            P(every, None, None),
            P(every),
        ),
        out_specs=(P("gx", yz), P("gx", yz), P(every, None)),
        check_vma=False,
    )
```

time: 116 us -> 119 us (1.026)
  Pallas kernels: 18.3 us -> 19.9 us
    pallas_call x1, Pallas kernels: 1.69 us -> 3.31 us  [attend(): pl.pallas_call(attend_kernel, in_specs=[pl.BlockSpec(memory_space=pltpu.S...]
    unnamed x10 -> x6, local copies, waits for them, and re-layouts: 3.13 us -> 3.38 us
    pallas_call x2 -> x3, Pallas kernels: 12.9 us -> 12.8 us  [the longest x1 7.14 us: project_ffn(): pl.pallas_call(ffn_kernel, in_specs=[pl.BlockSpec(memory_space=pltpu.HBM)...]
  transfers between devices with their start and end apart: 3 -> 3, of which waited for: 2 -> 2; matrix products, arithmetic and copies ran while one was open for 0% -> 1% of each run, Pallas kernels for 4% -> 9%
where the time goes in v3:
time: 119 us; the launch traced here: 118 us
  starting transfers between devices  31.5 us (26%)
  waiting for transfers between devices  27 us (23%)
  blocking collectives  20.9 us (18%)
  Pallas kernels  19.9 us (17%)
  between operations  14.7 us (12%)
  local copies, waits for them, and re-layouts  3.38 us (3%)
    all_to_all x1, waiting for transfers between devices, on_device(): part = lax.all_to_all(part, 'gx', 0, 0, tiled=True)  18.3 us
    all_to_all x1, starting transfers between devices, on_device(): feats = lax.all_to_all(mine, ('x', 'y', 'c'), 0, 0, tiled=True)  15.7 us
    all_to_all x1, starting transfers between devices, on_device(): part = lax.all_to_all(part, 'gx', 0, 0, tiled=True)  15.7 us
    all_to_all x1, blocking collectives, on_device(): context = lax.all_to_all(context, ('x', 'y'), 0, 0, tiled=True)  15.6 us
    all_to_all x1, waiting for transfers between devices, on_device(): feats = lax.all_to_all(mine, ('x', 'y', 'c'), 0, 0, tiled=True)  8.73 us
    pallas_call x1, Pallas kernels, project_ffn(): pl.pallas_call(ffn_kernel, in_specs=[pl.BlockSpec(memory_space=pltpu.HBM)...  7.14 us
    all_gather x1, blocking collectives, on_device(): context = lax.all_gather(context, 'c', axis=0, tiled=True)  5.34 us
    pallas_call x1, Pallas kernels, project_qkv(): pl.pallas_call(qkv_kernel, in_specs=[pl.BlockSpec(memory_space=pltpu.HBM)...  3.91 us
  transfers between devices with their start and end apart: 3, of which 2 were waited for; matrix products, arithmetic and copies ran while one was open for 1% of the time, Pallas kernels for 9%

profile of v3, /device:TPU:1, one launch (start us, length us, event | category | flops | bytes accessed | tf_op | source)
XLA Modules:
  0.0 118.1 jit_solution(10534677054700059901)
XLA Ops:
  7.2 0.0 reduce-scatter.2.cloned.1.call-start
  7.2 7.1 %project_ffn.1 = bf16[768,1152]{1,0:T(8,128)(2,1)} custom-call(bf16[768,1536]{1,0:T(8,128)(2,1)} %tok_hbm.3, bf16[576,1536]{1,0:T(8,128)(2,1)} %bitcast.17, bf16[576,1536]{1,0:T(8,128)(2,1)} %bitcast.18), custom_call_target="tpu_custom_call" | custom-call | flops 2717908992 | bytes 10000000 | tf_op jit(solution)/shard_map/project_ffn/pallas_call | solution.py:124
  14.4 0.0 reduce-scatter.2.cloned.1.call-update
  14.4 3.9 %project_qkv.1 = f32[768,128]{1,0:T(8,128)} custom-call(bf16[768,1536]{1,0:T(8,128)(2,1)} %tok_hbm.3, bf16[104,1536]{1,0:T(8,128)(2,1)} %bitcast.14), custom_call_target="tpu_custom_call" | custom-call | tf_op jit(solution)/shard_map/project_qkv/pallas_call | solution.py:67
  18.3 15.7 %all-to-all-start = ((f32[12,64,128]{2,1,0:T(8,128)}), f32[12,64,128]{2,1,0:T(8,128)S(1)}, u32[]{:S(2)}, u32[]{:S(2)}) async-start(f32[12,64,128]{2,1,0:T(8,128)} %bitcast.13), calls=%async_computation | async-start | bytes 786432 | tf_op jit(solution)/shard_map/all_to_all | solution.py:303
  34.6 0.1 fusion
  34.7 18.3 %all-to-all-done = f32[12,64,128]{2,1,0:T(8,128)S(1)} async-done(((f32[12,64,128]{2,1,0:T(8,128)}), f32[12,64,128]{2,1,0:T(8,128)S(1)}, u32[]{:S(2)}, u32[]{:S(2)}) %all-to-all-start) | async-done | bytes 393248 | tf_op jit(solution)/shard_map/all_to_all | solution.py:303
  53.0 0.0 copy-start.1
  53.0 0.8 copy-done.1
  53.8 1.8 %norm.1.feat_ref = f32[64,128]{1,0:T(8,128)} custom-call(f32[768,128]{1,0:T(8,128)} %bitcast.12), custom_call_target="tpu_custom_call" | custom-call | tf_op jit(solution)/shard_map/norm/pallas_call | solution.py:160
  55.5 15.7 %all-to-all-start.1 = ((f32[64,1,128]{2,1,0:T(1,128)}), f32[64,1,128]{2,1,0:T(1,128)S(1)}, u32[]{:S(2)}, u32[]{:S(2)}) async-start(f32[64,1,128]{2,1,0:T(1,128)} %bitcast.15), calls=%async_computation.1 | async-start | bytes 65536 | tf_op jit(solution)/shard_map/all_to_all | solution.py:307
  71.3 0.6 pad_maximum_fusion.turn_hbm
  71.9 8.7 %all-to-all-done.1 = f32[64,1,128]{2,1,0:T(1,128)S(1)} async-done(((f32[64,1,128]{2,1,0:T(1,128)}), f32[64,1,128]{2,1,0:T(1,128)S(1)}, u32[]{:S(2)}, u32[]{:S(2)}) %all-to-all-start.1) | async-done | bytes 32800 | tf_op jit(solution)/shard_map/all_to_all | solution.py:307
  80.6 0.0 copy-start.2
  80.6 0.6 copy-done.2
  81.2 3.3 %attend.1 = (bf16[32,48,128]{2,1,0:T(8,128)(2,1)}, bf16[1,512]{1,0:T(2,128)(2,1)}) custom-call(s32[1]{0:T(128)S(6)} %copy.12.len_ref, f32[64,128]{1,0:T(8,128)} %bitcast.16, f32[2,128]{1,0:T(2,128)} %pad_maximum_fusion.turn_hbm, bf16[1,512,256]{2,1,0:T(8,128)(2,1)} %key_hbm.1, bf16[1,512,256]{2,1,0:T(8,128)(2,1)} %value_hbm.1), custom_call_target="tpu_custom_call" | custom-call | tf_op jit(solution)/shard_map/attend/pallas_call | solution.py:231
  84.5 15.6 %all_to_all.27 = bf16[32,48,128]{2,1,0:T(8,128)(2,1)S(1)} all-to-all(bf16[32,48,128]{2,1,0:T(8,128)(2,1)} %get-tuple-element.5), channel_id=1, replica_groups=mesh['gx'=12,'x'=4,'y'=8,'c'=2] {'x','y'}, dimensions={0} | all-to-all | bytes 786432 | tf_op jit(solution)/shard_map/all_to_all | solution.py:309
  100.1 5.3 %all_gather.3.ctx_ref = bf16[64,48,128]{2,1,0:T(8,128)(2,1)S(1)} all-gather(bf16[32,48,128]{2,1,0:T(8,128)(2,1)S(1)} %all_to_all.27), channel_id=1, replica_groups=mesh['gx'=12,'x'=4,'y'=8,'c'=2] {'c'}, dimensions={0}, use_global_device_ids=true | all-gather | bytes 1179648 | tf_op jit(solution)/shard_map/all_gather | solution.py:310
  105.5 0.0 copy-start
  105.5 2.0 %copy-done = bf16[6144,288]{0,1:T(8,128)(2,1)S(1)} copy-done((bf16[6144,288]{0,1:T(8,128)(2,1)S(1)}, bf16[6144,288]{0,1:T(8,128)(2,1)}, u32[]{:S(2)}) %copy-start) | copy-done | bytes 3538968
  107.5 2.0 %output.1 = bf16[64,288]{1,0:T(8,128)(2,1)} custom-call(bf16[64,48,128]{2,1,0:T(8,128)(2,1)S(1)} %all_gather.3.ctx_ref, bf16[288,6144]{1,0:T(8,128)(2,1)S(1)} %bitcast.11), custom_call_target="tpu_custom_call" | custom-call | tf_op jit(solution)/shard_map/output/pallas_call | solution.py:267
  109.5 0.0 reduce-scatter.2.cloned.1.call-done.ffn_ref
  109.5 1.7 %hidden.1 = bf16[64,576]{1,0:T(8,128)(2,1)} custom-call(bf16[64,1152]{1,0:T(8,128)(2,1)} %reduce-scatter.2.cloned.1.call-done.ffn_ref, f32[64,128]{1,0:T(8,128)} %norm.1.feat_ref), custom_call_target="tpu_custom_call" | custom-call | tf_op jit(solution)/shard_map/hidden/pallas_call | solution.py:288
Async XLA Ops:
  7.2 102.3 %reduce-scatter.2.cloned.1.call-start = ((), (), s32[]{:S(2)}) async-start(), calls=%async_computation.4 | async-start | bytes 1916928 | tf_op jit(solution)/shard_map/reduce_scatter | solution.py:305
  18.3 34.7 %all-to-all-start = ((f32[12,64,128]{2,1,0:T(8,128)}), f32[12,64,128]{2,1,0:T(8,128)S(1)}, u32[]{:S(2)}, u32[]{:S(2)}) async-start(f32[12,64,128]{2,1,0:T(8,128)} %bitcast.13), calls=%async_computation | async-start | bytes 786432 | tf_op jit(solution)/shard_map/all_to_all | solution.py:303
  53.0 0.8 copy-start.1
  55.5 25.0 %all-to-all-start.1 = ((f32[64,1,128]{2,1,0:T(1,128)}), f32[64,1,128]{2,1,0:T(1,128)S(1)}, u32[]{:S(2)}, u32[]{:S(2)}) async-start(f32[64,1,128]{2,1,0:T(1,128)} %bitcast.15), calls=%async_computation.1 | async-start | bytes 65536 | tf_op jit(solution)/shard_map/all_to_all | solution.py:307
  80.6 0.6 copy-start.2
  105.5 2.0 %copy-start = (bf16[6144,288]{0,1:T(8,128)(2,1)S(1)}, bf16[6144,288]{0,1:T(8,128)(2,1)}, u32[]{:S(2)}) copy-start(bf16[6144,288]{0,1:T(8,128)(2,1)} %param.12) | copy-start | bytes 10616836
Sparse Core Ops, SparseCore 0:
  14.5 66.2 reduce-scatter.1
